TPU v7x, 32 devices: a whole 2x2x4 slice. The times are simulated.
32 devices in a mesh: groups: 2 (over x), queue: 16 (over z, y, core).
Axes of the slice: x: 2, y: 2, z: 4, core: 2. Of those that a mesh axis runs over, the one named last changes fastest.
Arguments:
- query: bfloat16 [32, 768, 2560], P(('groups', 'queue')), parts along dimension 0, may hold values from -6 to 6
- keys: bfloat16 [32, 768, 2560], P(('groups', 'queue')), parts along dimension 0, may hold values from -6 to 6
- values: bfloat16 [32, 768, 2560], P(('groups', 'queue')), parts along dimension 0, may hold values from -6 to 6
- gate_table: float32 [50, 2, 2560], replicated, may hold values from 0.5 to 2
- levels: int32 [32], P('groups'), parts along dimension 0, may hold values from 0 to 49
- window: int32 [32], P('groups'), parts along dimension 0, may hold values from 0 to 2, as said below
- queue_head: int32 [2], P('groups'), parts along dimension 0, may hold values from 1 to 15
Outputs:
- attended: bfloat16 [32, 768, 2560], P(('groups', 'queue')), parts along dimension 0
There are 2 independent parts, one for each index of `groups`. A program takes and returns all parts, laid end to end along the dimension named above; an argument that names none is the same for every part. Nothing has to cross between parts.
Inputs may be any that keep to these rules, and one draw needn't show every extreme that they name: `window`: at least one slot has width 2.
All inputs are finite; a program needn't handle non-finite values.
Results may differ from a plain program's by a relative error of at most 0.008.
Values may be sent and summed in bfloat16 or wider, within the bound.
A program may use at most 192 MiB of HBM per device.

v0:
```python
import math

import jax
import jax.numpy as jnp
from jax import lax
from jax.sharding import PartitionSpec as P

HEADS = 20
HEAD_DIM = 128
REACH = 2


def passed_along(value, axis, steps):
    count = lax.axis_size(axis)
    pairs = [(source, (source + steps) % count) for source in range(count)]
    return lax.ppermute(value, axis, pairs)


def spatial_frame(query_f, keys_f, values_f):
    tokens_here = query_f.shape[0]
    head_groups = math.gcd(HEADS, 4)
    per_group = HEADS // head_groups
    span_cols = per_group * HEAD_DIM
    score_scale = 1.0 / math.sqrt(HEAD_DIM)
    pieces = []
    for group_index in range(head_groups):
        lower = group_index * span_cols
        q_part = query_f[:, lower : lower + span_cols].reshape(tokens_here, per_group, HEAD_DIM)
        k_part = keys_f[:, lower : lower + span_cols].reshape(tokens_here, per_group, HEAD_DIM)
        v_part = values_f[:, lower : lower + span_cols].reshape(tokens_here, per_group, HEAD_DIM)
        scores = (
            jnp.einsum("qhd,khd->hqk", q_part, k_part, preferred_element_type=jnp.float32)
            * score_scale
        )
        top_score = jnp.max(scores, axis=-1, keepdims=True)
        expd = jnp.exp(scores - top_score)
        weights = (expd / jnp.sum(expd, axis=-1, keepdims=True)).astype(jnp.bfloat16)
        mixed_part = jnp.einsum("hqk,khd->qhd", weights, v_part, preferred_element_type=jnp.float32)
        pieces.append(mixed_part.reshape(tokens_here, span_cols))
    return jnp.concatenate(pieces, axis=1)


def temporal_blend(query_own, key_list, value_list, valid_list):
    lead = query_own.shape[:-1]
    score_scale = 1.0 / math.sqrt(HEAD_DIM)
    query_four = query_own.reshape(lead + (HEADS, HEAD_DIM))
    score_list = []
    for index in range(len(key_list)):
        near_keys = key_list[index].reshape(lead + (HEADS, HEAD_DIM))
        scores = (
            jnp.einsum(
                "...hd,...hd->...h", query_four, near_keys, preferred_element_type=jnp.float32
            )
            * score_scale
        )
        score_list.append(jnp.where(valid_list[index], scores, -1e30))
    stacked = jnp.stack(score_list)
    top_score = jnp.max(stacked, axis=0)
    expd = jnp.exp(stacked - top_score[None])
    weights = expd / jnp.sum(expd, axis=0)[None]
    result = jnp.zeros(lead + (HEADS, HEAD_DIM), jnp.float32)
    for index in range(len(value_list)):
        result = result + weights[index][..., None] * value_list[index].reshape(
            lead + (HEADS, HEAD_DIM)
        )
    return result.astype(jnp.bfloat16).reshape(query_own.shape)


def body(query, keys, values, gate_table, levels, window, queue_head):
    own_slot = lax.axis_index("queue")
    slot_count = lax.axis_size("queue")
    width_all = query.shape[2]
    slot_ids = jnp.arange(slot_count, dtype=jnp.int32)
    positions = (slot_ids - queue_head[0]) % slot_count
    own_position = jnp.sum(jnp.where(slot_ids == own_slot, positions, 0))
    own_window = jnp.sum(jnp.where(slot_ids == own_slot, window, 0))
    own_level = jnp.sum(jnp.where(slot_ids == own_slot, levels, 0))
    key_list = []
    value_list = []
    valid_list = []
    for offset in range(-REACH, REACH + 1):
        if offset == 0:
            pair = (keys[0], values[0])
        else:
            pair = passed_along((keys[0], values[0]), "queue", -offset)
        key_list.append(pair[0])
        value_list.append(pair[1])
        valid_list.append(
            (abs(offset) <= own_window)
            & (own_position + offset >= 0)
            & (own_position + offset < slot_count)
        )
    temporal = temporal_blend(query[0], key_list, value_list, valid_list)
    spatial = spatial_frame(query[0], keys[0], values[0])
    level_count = gate_table.shape[0]
    one_hot = (jnp.arange(level_count, dtype=jnp.int32) == own_level).astype(jnp.float32)
    gates = jnp.dot(
        one_hot[None, :],
        gate_table.reshape(level_count, 2 * width_all),
        precision=lax.Precision.HIGHEST,
    ).reshape(2, width_all)
    blended = gates[0][None, :] * spatial + gates[1][None, :] * temporal.astype(jnp.float32)
    return blended.astype(jnp.bfloat16)[None]


def solution(mesh):
    in_specs = (
        P(("groups", "queue"), None, None),
        P(("groups", "queue"), None, None),
        P(("groups", "queue"), None, None),
        P(),
        P("groups"),
        P("groups"),
        P("groups"),
    )
    out_specs = P(("groups", "queue"), None, None)
    return jax.shard_map(body, mesh=mesh, in_specs=in_specs, out_specs=out_specs, check_vma=False)
```

profile of v0, /device:TPU:0, one launch (start us, length us, event | category | flops | bytes accessed | tf_op | source)
XLA Modules:
  0.0 537.4 jit_solution(7058245112974914579)
XLA Ops:
  0.0 6.3 %copy.21 = bf16[1,768,2560]{1,2,0:T(8,128)(2,1)} copy(bf16[1,768,2560]{2,1,0:T(8,128)(2,1)} %param.8) | data formatting | bytes 7864320 | tf_op args[1]
  6.3 3.0 collective-permute-start
  9.2 0.0 collective-permute-start.1
  9.3 4.4 collective-permute-start.2
  13.7 0.4 collective-permute-start.3
  14.1 6.3 %copy.24 = bf16[1,768,2560]{1,2,0:T(8,128)(2,1)} copy(bf16[1,768,2560]{2,1,0:T(8,128)(2,1)} %param.9) | data formatting | bytes 7864320 | tf_op args[2]
  20.3 1.7 collective-permute-start.4
  22.0 3.7 fusion.58
  25.6 3.7 fusion.60
  29.4 6.3 %copy.20 = bf16[1,768,2560]{1,2,0:T(8,128)(2,1)} copy(bf16[1,768,2560]{2,1,0:T(8,128)(2,1)} %param.7) | data formatting | bytes 7864320 | tf_op args[0]
  35.7 4.1 fusion.59
  39.8 9.3 %fusion.64 = (f32[5,768]{1,0:T(8,128)S(1)}, f32[5,768,768]{1,2,0:T(8,128)}) fusion(bf16[768,5,128]{0,2,1:T(8,128)(2,1)} %bitcast.150, bf16[768,5,128]{0,2,1:T(8,128)(2,1)S(1)} %bitcast.148), kind=kOutput, calls=%fused_computation.98 | convolution fusion | flops 763822848 | bytes 13777920 | tf_op jit(solution)/shard_map/sub | solution.py:36
  49.1 9.2 %fusion.65 = (f32[5,768]{1,0:T(8,128)S(1)}, f32[5,768,768]{1,2,0:T(8,128)}) fusion(bf16[768,5,128]{0,2,1:T(8,128)(2,1)} %bitcast.149, bf16[768,5,128]{0,2,1:T(8,128)(2,1)S(1)} %bitcast.146), kind=kOutput, calls=%fused_computation.99 | convolution fusion | flops 763822848 | bytes 13777920 | tf_op jit(solution)/shard_map/sub | solution.py:36
  58.3 5.8 %fusion.33 = f32[5,768,128]{1,2,0:T(8,128)S(1)} fusion(bf16[768,5,128]{0,2,1:T(8,128)(2,1)} %bitcast.147, f32[5,768,768]{1,2,0:T(8,128)} %get-tuple-element.34, f32[5,768]{1,0:T(8,128)S(1)} %get-tuple-element.33), kind=kOutput, calls=%fused_computation.48 | convolution fusion | flops 760872960 | bytes 14760960 | tf_op jit(solution)/shard_map/hqk,khd->qhd/dot_general | solution.py:38
  64.0 0.0 copy-done.5
  64.0 2.5 copy-done.9
  66.6 2.2 fusion.32
  68.8 9.8 %fusion.63 = (f32[5,768]{1,0:T(8,128)S(1)}, f32[5,768,768]{1,2,0:T(8,128)}) fusion(bf16[768,5,128]{0,2,1:T(8,128)(2,1)} %bitcast.145, bf16[768,5,128]{0,2,1:T(8,128)(2,1)} %bitcast.142), kind=kOutput, calls=%fused_computation.97 | convolution fusion | flops 763822848 | bytes 13777920 | tf_op jit(solution)/shard_map/sub | solution.py:36
  78.6 9.5 %fusion.62 = (f32[5,768]{1,0:T(8,128)S(1)}, f32[5,768,768]{1,2,0:T(8,128)}) fusion(bf16[768,5,128]{0,2,1:T(8,128)(2,1)} %bitcast.143, bf16[768,5,128]{0,2,1:T(8,128)(2,1)} %bitcast.141), kind=kOutput, calls=%fused_computation.96 | convolution fusion | flops 763822848 | bytes 13777920 | tf_op jit(solution)/shard_map/sub | solution.py:36
  88.7 0.0 copy-done.6
  88.7 0.7 fusion.51
  89.4 6.8 %fusion.34 = f32[5,768,128]{1,2,0:T(8,128)} fusion(bf16[768,5,128]{0,2,1:T(8,128)(2,1)S(1)} %bitcast.140, f32[5,768,768]{1,2,0:T(8,128)} %get-tuple-element.32, f32[5,768]{1,0:T(8,128)S(1)} %get-tuple-element.31), kind=kOutput, calls=%fused_computation.49 | convolution fusion | flops 760872960 | bytes 14760960 | tf_op jit(solution)/shard_map/hqk,khd->qhd/dot_general | solution.py:38
  96.2 0.0 copy-done.4
  96.2 2.0 copy-done.8
  98.1 2.3 fusion.35
  100.5 120.8 %collective-permute-done = bf16[768,2560]{0,1:T(8,128)(2,1)} collective-permute-done((bf16[768,2560]{0,1:T(8,128)(2,1)}, bf16[768,2560]{0,1:T(8,128)(2,1)}, u32[]{:S(2)}, u32[]{:S(2)}) %collective-permute-start) | collective-permute-done | bytes 3932192 | tf_op jit(solution)/shard_map/ppermute | solution.py:16
  221.3 0.0 collective-permute-start.5
  221.3 0.0 collective-permute-done.1
  221.3 4.4 collective-permute-start.6
  225.8 0.0 collective-permute-done.2
  225.8 125.2 %collective-permute-start.7 = (bf16[768,2560]{0,1:T(8,128)(2,1)}, bf16[768,2560]{0,1:T(8,128)(2,1)}, u32[]{:S(2)}, u32[]{:S(2)}) collective-permute-start(bf16[768,2560]{0,1:T(8,128)(2,1)} %bitcast.6), channel_id=1, source_target_pairs={{0,14},{1,15},{2,0},{3,1},{4,2},{5,3},{6,4},{7,5},{8,6},{9,7},{10,... | collective-permute-start | bytes 11796488 | tf_op jit(solution)/shard_map/ppermute | solution.py:16
  351.0 0.6 select_reduce_fusion.1
  357.2 0.0 copy-done.3
  357.2 0.4 pad.4
  357.6 0.2 copy.76
  357.8 1.0 fusion.46
  358.9 72.9 %collective-permute-done.3 = bf16[768,2560]{0,1:T(8,128)(2,1)} collective-permute-done((bf16[768,2560]{0,1:T(8,128)(2,1)}, bf16[768,2560]{0,1:T(8,128)(2,1)}, u32[]{:S(2)}, u32[]{:S(2)}) %collective-permute-start.3) | collective-permute-done | bytes 3932192 | tf_op jit(solution)/shard_map/ppermute | solution.py:16
  431.8 11.1 %fusion.12 = (f32[768,20]{0,1:T(8,128)S(1)}, f32[768,20]{0,1:T(8,128)S(1)}, f32[768,20]{0,1:T(8,128)S(1)}, f32[768,20]{0,1:T(8,128)S(1)}, f32[768,20]{0,1:T(8,128)S(1)}) fusion(bf16[768,20,128]{0,2,1:T(8,128)(2,1)} %bitcast.131, bf16[768,20,128]{0,2,1:T(8,128)(2,1)} %bitcast.35, bf16[768,20,128]{0,2,1:T(8,128)(2,1)} %bitcast.29, ...), kind=kLoop, calls=%fused_computation.29 | loop fusion | flops 31380480 | bytes 23900160 | tf_op jit(solution)/shard_map/...hd,...hd->...h/dot_general | solution.py:51
  443.1 0.1 maximum_maximum_fusion
  443.1 0.1 fusion.45
  443.2 0.1 fusion.44
  443.3 0.0 collective-permute-done.4
  443.3 0.0 collective-permute-done.5
  443.3 0.0 collective-permute-done.6
  443.3 75.6 %collective-permute-done.7 = bf16[768,2560]{0,1:T(8,128)(2,1)} collective-permute-done((bf16[768,2560]{0,1:T(8,128)(2,1)}, bf16[768,2560]{0,1:T(8,128)(2,1)}, u32[]{:S(2)}, u32[]{:S(2)}) %collective-permute-start.7) | collective-permute-done | bytes 3932192 | tf_op jit(solution)/shard_map/ppermute | solution.py:16
  518.9 0.0 copy-done.2
  518.9 12.2 %fusion.14 = bf16[768,2560]{0,1:T(8,128)(2,1)} fusion(f32[768,640]{0,1:T(8,128)S(1)} %bitcast.138, f32[768,640]{0,1:T(8,128)S(1)} %bitcast.137, f32[768,640]{0,1:T(8,128)S(1)} %bitcast.135, f32[768,640]{0,1:T(8,128)S(1)} %bitcast.136, bf16[768,2560]{0,1:T(8,128)(2,1)} %collective-permute-done.7, bf16[768,2560]{0,1:T(8,128)(2,1)} %collective-permute-done.6, ...), kind=kLoop, calls=%fused_computation.32 | loop fusion | flops 45219840 | bytes 31784960 | tf_op jit(solution)/shard_map/convert_element_type | solution.py:103
  531.1 6.3 %copy.37 = bf16[1,768,2560]{2,1,0:T(8,128)(2,1)} copy(bf16[1,768,2560]{1,2,0:T(8,128)(2,1)} %bitcast.132) | data formatting | bytes 7864320 | tf_op jit(solution)/shard_map/broadcast_in_dim | solution.py:103
  (20 shorter events, 0.1 us)
Async XLA Ops:
  6.3 215.0 %collective-permute-start = (bf16[768,2560]{0,1:T(8,128)(2,1)}, bf16[768,2560]{0,1:T(8,128)(2,1)}, u32[]{:S(2)}, u32[]{:S(2)}) collective-permute-start(bf16[768,2560]{0,1:T(8,128)(2,1)} %bitcast.124), channel_id=1, source_target_pairs={{0,2},{1,3},{2,4},{3,5},{4,6},{5,7},{6,8},{7,9},{8,10},{9,11},{10,... | collective-permute-start | bytes 11796488 | tf_op jit(solution)/shard_map/ppermute | solution.py:16
  9.2 212.1 %collective-permute-start.1 = (bf16[768,2560]{0,1:T(8,128)(2,1)}, bf16[768,2560]{0,1:T(8,128)(2,1)}, u32[]{:S(2)}, u32[]{:S(2)}) collective-permute-start(bf16[768,2560]{0,1:T(8,128)(2,1)} %bitcast.125), channel_id=1, source_target_pairs={{0,1},{1,2},{2,3},{3,4},{4,5},{5,6},{6,7},{7,8},{8,9},{9,10},{10,1... | collective-permute-start | bytes 11796488 | tf_op jit(solution)/shard_map/ppermute | solution.py:16
  9.3 216.5 %collective-permute-start.2 = (bf16[768,2560]{0,1:T(8,128)(2,1)}, bf16[768,2560]{0,1:T(8,128)(2,1)}, u32[]{:S(2)}, u32[]{:S(2)}) collective-permute-start(bf16[768,2560]{0,1:T(8,128)(2,1)} %bitcast.126), channel_id=1, source_target_pairs={{0,15},{1,0},{2,1},{3,2},{4,3},{5,4},{6,5},{7,6},{8,7},{9,8},{10,9... | collective-permute-start | bytes 11796488 | tf_op jit(solution)/shard_map/ppermute | solution.py:16
  13.7 418.1 %collective-permute-start.3 = (bf16[768,2560]{0,1:T(8,128)(2,1)}, bf16[768,2560]{0,1:T(8,128)(2,1)}, u32[]{:S(2)}, u32[]{:S(2)}) collective-permute-start(bf16[768,2560]{0,1:T(8,128)(2,1)} %bitcast.127), channel_id=1, source_target_pairs={{0,14},{1,15},{2,0},{3,1},{4,2},{5,3},{6,4},{7,5},{8,6},{9,7},{10,... | collective-permute-start | bytes 11796488 | tf_op jit(solution)/shard_map/ppermute | solution.py:16
  20.3 423.0 %collective-permute-start.4 = (bf16[768,2560]{0,1:T(8,128)(2,1)}, bf16[768,2560]{0,1:T(8,128)(2,1)}, u32[]{:S(2)}, u32[]{:S(2)}) collective-permute-start(bf16[768,2560]{0,1:T(8,128)(2,1)} %bitcast.6), channel_id=1, source_target_pairs={{0,2},{1,3},{2,4},{3,5},{4,6},{5,7},{6,8},{7,9},{8,10},{9,11},{10,... | collective-permute-start | bytes 11796488 | tf_op jit(solution)/shard_map/ppermute | solution.py:16
  58.3 5.8 %copy-start.5 = (bf16[768,640]{0,1:T(8,128)(2,1)S(1)}, bf16[768,640]{0,1:T(8,128)(2,1)}, u32[]{:S(2)}) copy-start(bf16[768,640]{0,1:T(8,128)(2,1)} %get-tuple-element.18) | copy-start | bytes 2949124
  58.3 8.3 %copy-start.9 = (f32[5,768,768]{1,2,0:T(8,128)S(1)}, f32[5,768,768]{1,2,0:T(8,128)}, u32[]{:S(2)}) copy-start(f32[5,768,768]{1,2,0:T(8,128)} %get-tuple-element.36) | copy-start | bytes 35389444
  78.6 10.1 %copy-start.6 = (s32[16]{0:T(128)S(1)}, s32[16]{0:T(128)}, u32[]{:S(2)}) copy-start(s32[16]{0:T(128)} %param.12) | copy-start | bytes 196
  89.4 6.8 %copy-start.4 = (bf16[768,640]{0,1:T(8,128)(2,1)S(1)}, bf16[768,640]{0,1:T(8,128)(2,1)}, u32[]{:S(2)}) copy-start(bf16[768,640]{0,1:T(8,128)(2,1)} %get-tuple-element.19) | copy-start | bytes 2949124
  89.4 8.7 %copy-start.8 = (f32[5,768,768]{1,2,0:T(8,128)S(1)}, f32[5,768,768]{1,2,0:T(8,128)}, u32[]{:S(2)}) copy-start(f32[5,768,768]{1,2,0:T(8,128)} %get-tuple-element.30) | copy-start | bytes 35389444
  98.1 252.9 %copy-start.7 = (s32[16]{0:T(128)S(1)}, s32[16]{0:T(128)}, u32[]{:S(2)}) copy-start(s32[16]{0:T(128)} %param.11) | copy-start | bytes 196
  98.1 259.1 %copy-start.3 = (f32[50,2,2560]{2,1,0:T(2,128)S(1)}, f32[50,2,2560]{2,1,0:T(2,128)}, u32[]{:S(2)}) copy-start(f32[50,2,2560]{2,1,0:T(2,128)} %param.10) | copy-start | bytes 3072004
  221.3 222.0 %collective-permute-start.5 = (bf16[768,2560]{0,1:T(8,128)(2,1)}, bf16[768,2560]{0,1:T(8,128)(2,1)}, u32[]{:S(2)}, u32[]{:S(2)}) collective-permute-start(bf16[768,2560]{0,1:T(8,128)(2,1)} %bitcast.6), channel_id=1, source_target_pairs={{0,1},{1,2},{2,3},{3,4},{4,5},{5,6},{6,7},{7,8},{8,9},{9,10},{10,1... | collective-permute-start | bytes 11796488 | tf_op jit(solution)/shard_map/ppermute | solution.py:16
  221.3 222.0 %collective-permute-start.6 = (bf16[768,2560]{0,1:T(8,128)(2,1)}, bf16[768,2560]{0,1:T(8,128)(2,1)}, u32[]{:S(2)}, u32[]{:S(2)}) collective-permute-start(bf16[768,2560]{0,1:T(8,128)(2,1)} %bitcast.6), channel_id=1, source_target_pairs={{0,15},{1,0},{2,1},{3,2},{4,3},{5,4},{6,5},{7,6},{8,7},{9,8},{10,9... | collective-permute-start | bytes 11796488 | tf_op jit(solution)/shard_map/ppermute | solution.py:16
  225.8 293.1 %collective-permute-start.7 = (bf16[768,2560]{0,1:T(8,128)(2,1)}, bf16[768,2560]{0,1:T(8,128)(2,1)}, u32[]{:S(2)}, u32[]{:S(2)}) collective-permute-start(bf16[768,2560]{0,1:T(8,128)(2,1)} %bitcast.6), channel_id=1, source_target_pairs={{0,14},{1,15},{2,0},{3,1},{4,2},{5,3},{6,4},{7,5},{8,6},{9,7},{10,... | collective-permute-start | bytes 11796488 | tf_op jit(solution)/shard_map/ppermute | solution.py:16
  431.8 87.1 %copy-start = (f32[5,768,128]{1,2,0:T(8,128)S(1)}, f32[5,768,128]{1,2,0:T(8,128)}, u32[]{:S(2)}) copy-start(f32[5,768,128]{1,2,0:T(8,128)} %fusion.32) | copy-start | bytes 5898244
  431.8 87.1 %copy-start.1 = (f32[5,768,128]{1,2,0:T(8,128)S(1)}, f32[5,768,128]{1,2,0:T(8,128)}, u32[]{:S(2)}) copy-start(f32[5,768,128]{1,2,0:T(8,128)} %fusion.34) | copy-start | bytes 5898244
  431.8 87.1 %copy-start.2 = (f32[5,768,128]{1,2,0:T(8,128)S(1)}, f32[5,768,128]{1,2,0:T(8,128)}, u32[]{:S(2)}) copy-start(f32[5,768,128]{1,2,0:T(8,128)} %fusion.35) | copy-start | bytes 5898244
where the time goes:
time: 538 us; the launch traced here: 537 us
  waiting for transfers between devices  269 us (50%)
  starting transfers between devices  139 us (26%)
  matrix products  55.9 us (10%)
  local copies, waits for them, and re-layouts  41.8 us (8%)
  other arithmetic  24.9 us (5%)
  between operations  6.42 us (1%)
    ppermute x8, waiting for transfers between devices, passed_along(): return lax.ppermute(value, axis, pairs)  269 us
    ppermute x8, starting transfers between devices, passed_along(): return lax.ppermute(value, axis, pairs)  139 us
    sub x4, matrix products, spatial_frame(): expd = jnp.exp(scores - top_score)  37.7 us
    unnamed x25, local copies, waits for them, and re-layouts  24 us
    dot_general x4, matrix products, spatial_frame(): jnp.einsum('hqk,khd->qhd', weights, v_part, preferred_element_type=jnp.fl...  17.1 us
    convert_element_type x1, other arithmetic, body(): return blended.astype(jnp.bfloat16)[None]  12.2 us
    dot_general x1, other arithmetic, temporal_blend(): jnp.einsum('...hd,...hd->...h', query_four, near_keys, preferred_element_...  11.1 us
  transfers between devices with their start and end apart: 8, of which 3 were waited for; matrix products, arithmetic and copies ran while one was open for 17% of the time, Pallas kernels for 0%

commit v1 on v0

v1 whole, which is shorter than its diff:
```python
import functools
import math

import jax
import jax.numpy as jnp
from jax import lax
from jax.experimental import pallas as pl
from jax.experimental.pallas import tpu as pltpu
from jax.sharding import PartitionSpec as P

HEAD_DIM = 128
REACH = 2
TEAM = 4
CHUNK_HEADS = 2
ROW_BLOCK = 256
AHEAD = 2
LAG_TEMPORAL = 1
LAG_BLEND = 1
K, V, Q = 0, 1, 2


def kernel(
    n,
    levels_ref,
    window_ref,
    head_ref,
    gate_ref,
    q_hbm,
    k_hbm,
    v_hbm,
    out_hbm,
    own,
    swap,
    spatial,
    back,
    load_sem,
    swap_send,
    swap_recv,
    swap_local,
    halo_send,
    halo_recv,
    back_send,
    back_recv,
    back_local,
    out_sem,
):
    tokens, width = back.shape
    quarter = tokens // TEAM
    chunk = CHUNK_HEADS * HEAD_DIM
    count = width // chunk
    coef = math.log2(math.e) / math.sqrt(HEAD_DIM)

    slot = lax.axis_index("queue")
    place = lax.rem(slot, TEAM)
    team = slot - place
    following = lax.rem(slot + TEAM, n)
    previous = lax.rem(slot + n - TEAM, n)

    def cols(c):
        return pl.ds(pl.multiple_of(c * chunk, chunk), chunk)

    def rows(p):
        return pl.ds(pl.multiple_of(p * quarter, quarter), quarter)

    def loads(c):
        return [
            pltpu.make_async_copy(
                src.at[0, :, cols(c)], own.at[a, :, cols(c)], load_sem.at[c, a]
            )
            for a, src in ((K, k_hbm), (V, v_hbm), (Q, q_hbm))
        ]

    def swaps(c):
        copies = []
        for d in range(1, TEAM):
            peer = lax.rem(place + d, TEAM)
            copies.append(
                pltpu.make_async_remote_copy(
                    src_ref=own.at[:, rows(peer), cols(c)],
                    dst_ref=swap.at[place + REACH, :, :, cols(c)],
                    send_sem=swap_send.at[c, d - 1],
                    recv_sem=swap_recv.at[c, d - 1],
                    device_id={"queue": team + peer},
                    device_id_type=pl.DeviceIdType.MESH,
                )
            )
        return copies

    def swap_own(c):
        return pltpu.make_async_copy(
            own.at[:, rows(place), cols(c)],
            swap.at[place + REACH, :, :, cols(c)],
            swap_local.at[c],
        )

    def halos(c):
        copies = []
        for way, src, dst, target in (
            (0, TEAM, 0, following),
            (1, REACH, TEAM + REACH, previous),
        ):
            copies.append(
                pltpu.make_async_remote_copy(
                    src_ref=swap.at[pl.ds(src, REACH), pl.ds(0, 2), :, cols(c)],
                    dst_ref=swap.at[pl.ds(dst, REACH), pl.ds(0, 2), :, cols(c)],
                    send_sem=halo_send.at[c, way],
                    recv_sem=halo_recv.at[c, way],
                    device_id={"queue": target},
                    device_id_type=pl.DeviceIdType.MESH,
                )
            )
        return copies

    def result_at(j):
        return j + TEAM * (j // 2)

    def backs(c):
        copies = []
        for d in range(1, TEAM):
            peer = lax.rem(place + d, TEAM)
            copies.append(
                pltpu.make_async_remote_copy(
                    src_ref=swap.at[result_at(peer), Q, :, cols(c)],
                    dst_ref=back.at[rows(place), cols(c)],
                    send_sem=back_send.at[c, d - 1],
                    recv_sem=back_recv.at[c, d - 1],
                    device_id={"queue": team + peer},
                    device_id_type=pl.DeviceIdType.MESH,
                )
            )
        return copies

    def back_own(c):
        return pltpu.make_async_copy(
            swap.at[result_at(place), Q, :, cols(c)],
            back.at[rows(place), cols(c)],
            back_local.at[c],
        )

    def store_out(c):
        return pltpu.make_async_copy(
            back.at[:, cols(c)], out_hbm.at[0, :, cols(c)], out_sem.at[c]
        )

    def start_load(c, _):
        for copy in loads(c):
            copy.start()
        return 0

    def start_swap(c):
        for copy in loads(c):
            copy.wait()
        for copy in swaps(c):
            copy.start()
        swap_own(c).start()

    def head_cols(c, h):
        return pl.ds(pl.multiple_of(c * chunk + h * HEAD_DIM, HEAD_DIM), HEAD_DIM)

    level = levels_ref[slot]

    def do_spatial(c):
        for h in range(CHUNK_HEADS):
            hc = head_cols(c, h)
            keys = own[K, :, hc]
            vals = own[V, :, hc]
            vals = jnp.concatenate([vals, jnp.ones_like(vals)], axis=1)
            gate = gate_ref[level, 0:1, hc]
            for r in range(0, tokens, ROW_BLOCK):
                rs = pl.ds(r, ROW_BLOCK)
                s = lax.dot_general(
                    own[Q, rs, hc],
                    keys,
                    (((1,), (1,)), ((), ())),
                    preferred_element_type=jnp.float32,
                )
                top = jnp.max(s, axis=1, keepdims=True)
                e = jnp.exp2((s - top) * coef).astype(jnp.bfloat16)
                o = jnp.dot(e, vals, preferred_element_type=jnp.float32)
                spatial[rs, hc] = gate * (o[:, :HEAD_DIM] / o[:, HEAD_DIM:])

    def do_temporal(c):
        ones = jnp.ones((2 * HEAD_DIM, HEAD_DIM), jnp.bfloat16)

        def one_slot(j, _):
            at = team + j
            position = lax.rem(at - head_ref[0] + n, n)
            reach = window_ref[at]
            for h in range(CHUNK_HEADS):
                hc = head_cols(c, h)
                query = swap[j + REACH, Q, :, hc].astype(jnp.float32)
                scores = []
                for o in range(2 * REACH + 1):
                    offset = o - REACH
                    product = query * swap[j + o, K, :, hc].astype(jnp.float32)
                    high = product.astype(jnp.bfloat16)
                    low = (product - high.astype(jnp.float32)).astype(jnp.bfloat16)
                    s = (
                        jnp.dot(
                            jnp.concatenate([high, low], axis=1),
                            ones,
                            preferred_element_type=jnp.float32,
                        )
                        * coef
                    )
                    if offset:
                        valid = (
                            (reach >= abs(offset))
                            & (position + offset >= 0)
                            & (position + offset < n)
                        )
                        s = s + jnp.where(valid, 0.0, -1e30).astype(jnp.float32)
                    scores.append(s)
                top = functools.reduce(jnp.maximum, scores)
                total = 0.0
                mixed = 0.0
                for o in range(2 * REACH + 1):
                    e = jnp.exp2(scores[o] - top)
                    total = total + e
                    mixed = mixed + e * swap[j + o, V, :, hc].astype(jnp.float32)
                swap[result_at(j), Q, :, hc] = (mixed / total).astype(jnp.bfloat16)
            return 0

        lax.fori_loop(0, TEAM, one_slot, 0)

    def do_blend(c):
        for h in range(CHUNK_HEADS):
            hc = head_cols(c, h)
            gate = gate_ref[level, 1:2, hc]
            mixed = spatial[:, hc] + gate * back[:, hc].astype(jnp.float32)
            back[:, hc] = mixed.astype(jnp.bfloat16)

    lax.fori_loop(0, count, start_load, 0)
    barrier = pltpu.get_barrier_semaphore()
    mates = [team + lax.rem(place + d, TEAM) for d in range(1, TEAM)]
    for other in mates + [following, previous]:
        pl.semaphore_signal(
            barrier, inc=1, device_id={"queue": other}, device_id_type=pl.DeviceIdType.MESH
        )
    pl.semaphore_wait(barrier, TEAM + 1)

    def first(c, _):
        start_swap(c)
        return 0

    lax.fori_loop(0, AHEAD, first, 0)

    def step(i, _):
        @pl.when(i < count)
        def _():
            for copy in swaps(i):
                copy.wait_recv()
            swap_own(i).wait()
            for copy in halos(i):
                copy.start()

            @pl.when(i + AHEAD < count)
            def _():
                start_swap(i + AHEAD)

            do_spatial(i)

        t = i - LAG_TEMPORAL

        @pl.when((t >= 0) & (t < count))
        def _():
            for copy in halos(t):
                copy.wait_recv()
            do_temporal(t)
            for copy in backs(t):
                copy.start()
            back_own(t).start()

        b = t - LAG_BLEND

        @pl.when(b >= 0)
        def _():
            for copy in backs(b):
                copy.wait_recv()
            back_own(b).wait()
            do_blend(b)
            store_out(b).start()

        return 0

    lax.fori_loop(0, count + LAG_TEMPORAL + LAG_BLEND, step, 0)

    def finish(c, _):
        for copy in swaps(c) + halos(c) + backs(c):
            copy.wait_send()
        store_out(c).wait()
        return 0

    lax.fori_loop(0, count, finish, 0)


def body(query, keys, values, gate_table, levels, window, queue_head):
    n = lax.axis_size("queue")
    _, tokens, width = query.shape
    count = width // (CHUNK_HEADS * HEAD_DIM)
    dma = pltpu.SemaphoreType.DMA
    smem = pl.BlockSpec(memory_space=pltpu.SMEM)
    hbm = pl.BlockSpec(memory_space=pl.ANY)
    return pl.pallas_call(
        functools.partial(kernel, n),
        out_shape=jax.ShapeDtypeStruct(query.shape, jnp.bfloat16),
        in_specs=[smem, smem, smem, pl.BlockSpec(memory_space=pltpu.VMEM), hbm, hbm, hbm],
        out_specs=hbm,
        scratch_shapes=[
            pltpu.VMEM((3, tokens, width), jnp.bfloat16),
            pltpu.VMEM((TEAM + 2 * REACH, 3, tokens // TEAM, width), jnp.bfloat16),
            pltpu.VMEM((tokens, width), jnp.float32),
            pltpu.VMEM((tokens, width), jnp.bfloat16),
            dma((count, 3)),
            dma((count, TEAM - 1)),
            dma((count, TEAM - 1)),
            dma((count,)),
            dma((count, 2)),
            dma((count, 2)),
            dma((count, TEAM - 1)),
            dma((count, TEAM - 1)),
            dma((count,)),
            dma((count,)),
        ],
        compiler_params=pltpu.CompilerParams(
            collective_id=0, has_side_effects=True, vmem_limit_bytes=60 * 2**20
        ),
        cost_estimate=pl.CostEstimate(
            flops=4 * tokens * tokens * width,
            bytes_accessed=8 * tokens * width,
            transcendentals=tokens * tokens * width // HEAD_DIM,
        ),
    )(levels, window, queue_head, gate_table, query, keys, values)


def solution(mesh):
    spread = P(("groups", "queue"), None, None)
    in_specs = (spread, spread, spread, P(), P("groups"), P("groups"), P("groups"))
    return jax.shard_map(body, mesh=mesh, in_specs=in_specs, out_specs=spread, check_vma=False)
```

time: 538 us -> 200 us (0.37)
  waiting for transfers between devices: 269 us -> 0 us
  Pallas kernels: 0 us -> 195 us
  starting transfers between devices: 139 us -> 0 us
  matrix products: 55.9 us -> 0 us
  local copies, waits for them, and re-layouts: 41.8 us -> 4.29 us
  other arithmetic: 24.9 us -> 0 us
  between operations: 6.42 us -> 0.66 us
    ppermute x8 -> x0, waiting for transfers between devices: 269 us -> none  [passed_along(): return lax.ppermute(value, axis, pairs)]
    pallas_call x0 -> x1, Pallas kernels: none -> 195 us  [body(): pl.pallas_call(functools.partial(kernel, n), out_shape=jax.ShapeDtypeStru...]
    ppermute x8 -> x0, starting transfers between devices: 139 us -> none  [passed_along(): return lax.ppermute(value, axis, pairs)]
    sub x4 -> x0, matrix products: 37.7 us -> none  [spatial_frame(): expd = jnp.exp(scores - top_score)]
    unnamed x25 -> x1, local copies, waits for them, and re-layouts: 24 us -> 4.29 us
    dot_general x5 -> x0, matrix products: 18.2 us -> none  [the longest x4 17.1 us: spatial_frame(): jnp.einsum('hqk,khd->qhd', weights, v_part, preferred_element_type=jnp.fl...]
    convert_element_type x1 -> x0, other arithmetic: 12.2 us -> none  [body(): return blended.astype(jnp.bfloat16)[None]]
    slice x4 -> x0, local copies, waits for them, and re-layouts: 11.5 us -> none  [the longest x1 4.11 us: spatial_frame(): query_f[:, lower:lower + span_cols]]
  transfers between devices with their start and end apart: 8 -> 0, of which waited for: 3 -> 0; matrix products, arithmetic and copies ran while one was open for 17% -> 0% of each run, Pallas kernels for 0% -> 0%
where the time goes in v1:
time: 200 us
  Pallas kernels  195 us (98%)
  local copies, waits for them, and re-layouts  4.29 us (2%)
    pallas_call x1, Pallas kernels, body(): pl.pallas_call(functools.partial(kernel, n), out_shape=jax.ShapeDtypeStru...  195 us
    unnamed x1, local copies, waits for them, and re-layouts  4.29 us

profile of v1, /device:TPU:0, one launch (start us, length us, event | category | flops | bytes accessed | tf_op | source)
XLA Modules:
  0.0 199.6 jit_solution(8963802671131577407)
XLA Ops:
  0.7 194.6 %shard_map.73 = bf16[1,768,2560]{2,1,0:T(8,128)(2,1)} custom-call(s32[16]{0:T(128)} %levels_ref.1, s32[16]{0:T(128)} %window_ref.1, s32[1]{0:T(128)S(6)} %copy.9.head_ref, f32[50,2,2560]{2,1,0:T(2,128)} %gate_ref.1, bf16[1,768,2560]{2,1,0:T(8,128)(2,1)} %q_hbm.1, bf16[1,768,2560]{2,1,0:T(8,128)(2,1)} %k_hbm.1, bf16[1,768,2560]{2,1,0:T(8,128)(2,1)} %v_hbm.1), custom_call_target="tpu_custom_call" | custom-call | flops 6039797760 | bytes 15728640 | tf_op jit(solution)/shard_map/pallas_call | solution.py:304
  195.3 4.3 %copy.10 = bf16[1,768,2560]{2,1,0:T(8,128)(2,1)} copy(bf16[1,768,2560]{2,1,0:T(8,128)(2,1)} %shard_map.73) | data formatting | bytes 7864320

commit v2 on v1

--- a/solution.py
+++ b/solution.py
@@ -11,7 +11,7 @@
 HEAD_DIM = 128
 REACH = 2
 TEAM = 4
-CHUNK_HEADS = 2
+CHUNK_HEADS = 1
 ROW_BLOCK = 256
 AHEAD = 2
 LAG_TEMPORAL = 1
@@ -24,7 +24,7 @@
     levels_ref,
     window_ref,
     head_ref,
-    gate_ref,
+    gate_hbm,
     q_hbm,
     k_hbm,
     v_hbm,
@@ -32,11 +32,15 @@
     own,
     swap,
     spatial,
+    gate_ref,
     back,
+    gate_sem,
     load_sem,
     swap_send,
     swap_recv,
     swap_local,
+    direct_send,
+    direct_recv,
     halo_send,
     halo_recv,
     back_send,
@@ -53,8 +57,8 @@
     slot = lax.axis_index("queue")
     place = lax.rem(slot, TEAM)
     team = slot - place
-    following = lax.rem(slot + TEAM, n)
-    previous = lax.rem(slot + n - TEAM, n)
+    half = place // REACH
+    core = lax.rem(place, REACH)
 
     def cols(c):
         return pl.ds(pl.multiple_of(c * chunk, chunk), chunk)
@@ -70,16 +74,17 @@
             for a, src in ((K, k_hbm), (V, v_hbm), (Q, q_hbm))
         ]
 
-    def swaps(c):
+    def swaps(c, part):
+        arrays = pl.ds(0, 2) if part == 0 else pl.ds(Q, 1)
         copies = []
         for d in range(1, TEAM):
             peer = lax.rem(place + d, TEAM)
             copies.append(
                 pltpu.make_async_remote_copy(
-                    src_ref=own.at[:, rows(peer), cols(c)],
-                    dst_ref=swap.at[place + REACH, :, :, cols(c)],
-                    send_sem=swap_send.at[c, d - 1],
-                    recv_sem=swap_recv.at[c, d - 1],
+                    src_ref=own.at[arrays, rows(peer), cols(c)],
+                    dst_ref=swap.at[place + REACH, arrays, :, cols(c)],
+                    send_sem=swap_send.at[c, part, d - 1],
+                    recv_sem=swap_recv.at[c, part, d - 1],
                     device_id={"queue": team + peer},
                     device_id_type=pl.DeviceIdType.MESH,
                 )
@@ -93,23 +98,25 @@
             swap_local.at[c],
         )
 
-    def halos(c):
-        copies = []
-        for way, src, dst, target in (
-            (0, TEAM, 0, following),
-            (1, REACH, TEAM + REACH, previous),
-        ):
-            copies.append(
-                pltpu.make_async_remote_copy(
-                    src_ref=swap.at[pl.ds(src, REACH), pl.ds(0, 2), :, cols(c)],
-                    dst_ref=swap.at[pl.ds(dst, REACH), pl.ds(0, 2), :, cols(c)],
-                    send_sem=halo_send.at[c, way],
-                    recv_sem=halo_recv.at[c, way],
-                    device_id={"queue": target},
-                    device_id_type=pl.DeviceIdType.MESH,
-                )
-            )
-        return copies
+    def direct(c, target, source):
+        return pltpu.make_async_remote_copy(
+            src_ref=own.at[pl.ds(0, 2), rows(REACH * half + target), cols(c)],
+            dst_ref=swap.at[TEAM + REACH + source - 6 * half, pl.ds(0, 2), :, cols(c)],
+            send_sem=direct_send.at[c, target],
+            recv_sem=direct_recv.at[c, source],
+            device_id={"queue": lax.rem(slot - core + target + n + TEAM * (2 * half - 1), n)},
+            device_id_type=pl.DeviceIdType.MESH,
+        )
+
+    def halo(c):
+        return pltpu.make_async_remote_copy(
+            src_ref=swap.at[pl.ds(TEAM - REACH * half, REACH), pl.ds(0, 2), :, cols(c)],
+            dst_ref=swap.at[pl.ds(6 * half, REACH), pl.ds(0, 2), :, cols(c)],
+            send_sem=halo_send.at[c],
+            recv_sem=halo_recv.at[c],
+            device_id={"queue": lax.rem(slot + n + TEAM * (1 - 2 * half), n)},
+            device_id_type=pl.DeviceIdType.MESH,
+        )
 
     def result_at(j):
         return j + TEAM * (j // 2)
@@ -150,9 +157,15 @@
     def start_swap(c):
         for copy in loads(c):
             copy.wait()
-        for copy in swaps(c):
+        for copy in swaps(c, 0):
             copy.start()
+        for e in range(REACH):
+            direct(c, e, core).start()
         swap_own(c).start()
+
+    def start_queries(c):
+        for copy in swaps(c, 1):
+            copy.start()
 
     def head_cols(c, h):
         return pl.ds(pl.multiple_of(c * chunk + h * HEAD_DIM, HEAD_DIM), HEAD_DIM)
@@ -230,42 +243,54 @@
             mixed = spatial[:, hc] + gate * back[:, hc].astype(jnp.float32)
             back[:, hc] = mixed.astype(jnp.bfloat16)
 
-    lax.fori_loop(0, count, start_load, 0)
+    lax.fori_loop(0, AHEAD, start_load, 0)
+    gates = pltpu.make_async_copy(gate_hbm, gate_ref, gate_sem)
     barrier = pltpu.get_barrier_semaphore()
-    mates = [team + lax.rem(place + d, TEAM) for d in range(1, TEAM)]
-    for other in mates + [following, previous]:
+    others = [team + lax.rem(place + d, TEAM) for d in range(1, TEAM)]
+    for e in range(REACH):
+        others.append(lax.rem(slot - core + e + TEAM, n))
+        others.append(lax.rem(slot - core + e + n - TEAM, n))
+    for other in others:
         pl.semaphore_signal(
             barrier, inc=1, device_id={"queue": other}, device_id_type=pl.DeviceIdType.MESH
         )
-    pl.semaphore_wait(barrier, TEAM + 1)
-
-    def first(c, _):
+    pl.semaphore_wait(barrier, len(others))
+
+    for c in range(AHEAD):
         start_swap(c)
-        return 0
-
-    lax.fori_loop(0, AHEAD, first, 0)
+    lax.fori_loop(AHEAD, count, start_load, 0)
+    gates.start()
+    for c in range(AHEAD - 1):
+        start_queries(c)
+    gates.wait()
 
     def step(i, _):
         @pl.when(i < count)
         def _():
-            for copy in swaps(i):
+            for copy in swaps(i, 0):
                 copy.wait_recv()
             swap_own(i).wait()
-            for copy in halos(i):
-                copy.start()
+            halo(i).start()
 
             @pl.when(i + AHEAD < count)
             def _():
                 start_swap(i + AHEAD)
 
+            @pl.when(i + AHEAD - 1 < count)
+            def _():
+                start_queries(i + AHEAD - 1)
+
             do_spatial(i)
 
         t = i - LAG_TEMPORAL
 
         @pl.when((t >= 0) & (t < count))
         def _():
-            for copy in halos(t):
+            for copy in swaps(t, 1):
                 copy.wait_recv()
+            for e in range(REACH):
+                direct(t, e, e).wait_recv()
+            halo(t).wait_recv()
             do_temporal(t)
             for copy in backs(t):
                 copy.start()
@@ -286,8 +311,10 @@
     lax.fori_loop(0, count + LAG_TEMPORAL + LAG_BLEND, step, 0)
 
     def finish(c, _):
-        for copy in swaps(c) + halos(c) + backs(c):
+        for copy in swaps(c, 0) + swaps(c, 1) + backs(c) + [halo(c)]:
             copy.wait_send()
+        for e in range(REACH):
+            direct(c, e, core).wait_send()
         store_out(c).wait()
         return 0
 
@@ -304,19 +331,23 @@
     return pl.pallas_call(
         functools.partial(kernel, n),
         out_shape=jax.ShapeDtypeStruct(query.shape, jnp.bfloat16),
-        in_specs=[smem, smem, smem, pl.BlockSpec(memory_space=pltpu.VMEM), hbm, hbm, hbm],
+        in_specs=[smem, smem, smem, hbm, hbm, hbm, hbm],
         out_specs=hbm,
         scratch_shapes=[
             pltpu.VMEM((3, tokens, width), jnp.bfloat16),
             pltpu.VMEM((TEAM + 2 * REACH, 3, tokens // TEAM, width), jnp.bfloat16),
             pltpu.VMEM((tokens, width), jnp.float32),
+            pltpu.VMEM(gate_table.shape, jnp.float32),
             pltpu.VMEM((tokens, width), jnp.bfloat16),
+            dma,
             dma((count, 3)),
-            dma((count, TEAM - 1)),
-            dma((count, TEAM - 1)),
+            dma((count, 2, TEAM - 1)),
+            dma((count, 2, TEAM - 1)),
             dma((count,)),
             dma((count, 2)),
             dma((count, 2)),
+            dma((count,)),
+            dma((count,)),
             dma((count, TEAM - 1)),
             dma((count, TEAM - 1)),
             dma((count,)),

time: 200 us -> 193 us (0.965)
  Pallas kernels: 195 us -> 188 us
    pallas_call x1, Pallas kernels: 195 us -> 188 us  [body(): pl.pallas_call(functools.partial(kernel, n), out_shape=jax.ShapeDtypeStru...]
where the time goes in v2:
time: 193 us
  Pallas kernels  188 us (97%)
  local copies, waits for them, and re-layouts  4.29 us (2%)
    pallas_call x1, Pallas kernels, body(): pl.pallas_call(functools.partial(kernel, n), out_shape=jax.ShapeDtypeStru...  188 us
    unnamed x1, local copies, waits for them, and re-layouts  4.29 us

profile of v2, /device:TPU:0, one launch (start us, length us, event | category | flops | bytes accessed | tf_op | source)
XLA Modules:
  0.0 192.7 jit_solution(11784256949271987322)
XLA Ops:
  0.7 187.8 %shard_map.73 = bf16[1,768,2560]{2,1,0:T(8,128)(2,1)} custom-call(s32[16]{0:T(128)} %levels_ref.1, s32[16]{0:T(128)} %window_ref.1, s32[1]{0:T(128)S(6)} %copy.9.head_ref, f32[50,2,2560]{2,1,0:T(2,128)} %gate_hbm.1, bf16[1,768,2560]{2,1,0:T(8,128)(2,1)} %q_hbm.1, bf16[1,768,2560]{2,1,0:T(8,128)(2,1)} %k_hbm.1, bf16[1,768,2560]{2,1,0:T(8,128)(2,1)} %v_hbm.1), custom_call_target="tpu_custom_call" | custom-call | flops 6039797760 | bytes 15728640 | tf_op jit(solution)/shard_map/pallas_call | solution.py:331
  188.4 4.3 %copy.10 = bf16[1,768,2560]{2,1,0:T(8,128)(2,1)} copy(bf16[1,768,2560]{2,1,0:T(8,128)(2,1)} %shard_map.73) | data formatting | bytes 7864320

commit v3 on v2

--- a/solution.py
+++ b/solution.py
@@ -280,8 +280,6 @@
             def _():
                 start_queries(i + AHEAD - 1)
 
-            do_spatial(i)
-
         t = i - LAG_TEMPORAL
 
         @pl.when((t >= 0) & (t < count))
@@ -295,6 +293,10 @@
             for copy in backs(t):
                 copy.start()
             back_own(t).start()
+
+        @pl.when(i < count)
+        def _():
+            do_spatial(i)
 
         b = t - LAG_BLEND
 

time: 193 us -> 193 us (level)
  no operation moved by 1% of the time
where the time goes in v3:
time: 193 us
  Pallas kernels  188 us (97%)
  local copies, waits for them, and re-layouts  4.29 us (2%)
    pallas_call x1, Pallas kernels, body(): pl.pallas_call(functools.partial(kernel, n), out_shape=jax.ShapeDtypeStru...  188 us
    unnamed x1, local copies, waits for them, and re-layouts  4.29 us

profile of v3, /device:TPU:0, one launch (start us, length us, event | category | flops | bytes accessed | tf_op | source)
XLA Modules:
  0.0 192.7 jit_solution(16526089810523155880)
XLA Ops:
  0.7 187.8 %shard_map.73 = bf16[1,768,2560]{2,1,0:T(8,128)(2,1)} custom-call(s32[16]{0:T(128)} %levels_ref.1, s32[16]{0:T(128)} %window_ref.1, s32[1]{0:T(128)S(6)} %copy.9.head_ref, f32[50,2,2560]{2,1,0:T(2,128)} %gate_hbm.1, bf16[1,768,2560]{2,1,0:T(8,128)(2,1)} %q_hbm.1, bf16[1,768,2560]{2,1,0:T(8,128)(2,1)} %k_hbm.1, bf16[1,768,2560]{2,1,0:T(8,128)(2,1)} %v_hbm.1), custom_call_target="tpu_custom_call" | custom-call | flops 6039797760 | bytes 15728640 | tf_op jit(solution)/shard_map/pallas_call | solution.py:333
  188.4 4.3 %copy.10 = bf16[1,768,2560]{2,1,0:T(8,128)(2,1)} copy(bf16[1,768,2560]{2,1,0:T(8,128)(2,1)} %shard_map.73) | data formatting | bytes 7864320
